TPU v7x, 32 devices: a whole 2x2x4 slice. The times are simulated.
32 devices in a mesh: grp: 2 (over y), fib: 4 (over z), slab: 2 (over x), var: 2 (over core).
Axes of the slice: x: 2, y: 2, z: 4, core: 2. Of those that a mesh axis runs over, the one named last changes fastest.
Arguments:
- field: bfloat16 [32, 512, 64, 256], P(('grp', 'var'), 'fib', 'slab'), parts along dimension 0, may hold values from -800 to 800
- rank: int32 [32], P(('grp', 'var')), parts along dimension 0, may hold values from 32 to 128
- start_basis: float32 [512, 128], replicated, may hold values from -6 to 6
Outputs:
- rebuilt: bfloat16 [32, 512, 64, 256], P(('grp', 'var'), 'fib', 'slab'), parts along dimension 0
There are 2 independent parts, one for each index of `grp`. A program takes and returns all parts, laid end to end along the dimension named above; an argument that names none is the same for every part. Nothing has to cross between parts.
All inputs are finite; a program needn't handle non-finite values.
Results may differ from a plain program's by a relative error of at most 0.0062.
Values may be sent and summed in bfloat16 or wider, within the bound.
A program may use at most 192 MiB of HBM per device.

v0:
```python
import jax
import jax.numpy as jnp
from jax import lax
from jax.sharding import PartitionSpec as P

ITERS = 4


def orthonormal(block):
    small = jnp.dot(block.T, block, precision=lax.Precision.HIGHEST)
    factor = jnp.linalg.cholesky(small)
    return lax.linalg.triangular_solve(factor, block, left_side=False, lower=True, transpose_a=True)


def on_device(field, rank, start_basis):
    nvars, rows, depth, width = field.shape
    flat = field.reshape(nvars, rows, depth * width)
    fibres = lax.all_to_all(flat, "fib", split_axis=2, concat_axis=1, tiled=True)
    partial_value = jnp.einsum("vic,vjc->ij", fibres, fibres, preferred_element_type=jnp.float32)
    gram = lax.psum(partial_value, ("fib", "slab", "var"))
    basis = orthonormal(start_basis)
    for step in range(ITERS):
        basis = orthonormal(jnp.dot(gram, basis, precision=lax.Precision.HIGHEST))
    columns = jnp.arange(basis.shape[1], dtype=jnp.int32)
    keep = (columns[None, :] < rank[:, None]).astype(basis.dtype)
    basis_bf = (basis[None, :, :] * keep[:, None, :]).astype(jnp.bfloat16)
    core = jnp.einsum("vir,vic->vrc", basis_bf, fibres, preferred_element_type=jnp.float32).astype(
        jnp.bfloat16
    )
    own_rows = lax.dynamic_slice_in_dim(basis_bf, lax.axis_index("fib") * rows, rows, 1)
    result = jnp.einsum(
        "vir,vrc->vic",
        own_rows,
        lax.all_gather(core, "fib", axis=2, tiled=True),
        preferred_element_type=jnp.float32,
    ).astype(jnp.bfloat16)
    return result.reshape(nvars, rows, depth, width)


def solution(mesh):
    return jax.shard_map(
        on_device,
        mesh=mesh,
        in_specs=(P(("grp", "var"), "fib", "slab", None), P(("grp", "var")), P()),
        out_specs=P(("grp", "var"), "fib", "slab", None),
        check_vma=False,
    )
```

profile of v0, /device:TPU:0, one launch (start us, length us, event | category | flops | bytes accessed | tf_op | source)
XLA Modules:
  0.0 985.7 jit_solution(13465007174928289063)
XLA Ops:
  6.5 36.3 %copy.18 = bf16[8,128,32,256]{1,0,3,2:T(8,128)(2,1)} copy(bf16[8,128,32,256]{3,2,1,0:T(8,128)(2,1)} %param.6) | data formatting | bytes 33554432 | tf_op args[0]
  42.8 7.0 all-to-all-start
  50.6 11.7 %cholesky.89 = f32[128,128]{1,0:T(8,128)S(1)} custom-call(f32[128,128]{1,0:T(8,128)S(1)} %fusion.15), custom_call_target="Cholesky" | custom-call | tf_op jit(solution)/shard_map/jit(cholesky)/cholesky | solution.py:11
  63.0 351.4 %all-to-all-done = bf16[8,128,8192]{1,0,2:T(8,128)(2,1)} async-done(((bf16[8,128,8192]{1,0,2:T(8,128)(2,1)}), bf16[8,128,8192]{1,0,2:T(8,128)(2,1)}, u32[]{:S(2)}, u32[]{:S(2)}) %all-to-all-start) | async-done | bytes 16777248 | tf_op jit(solution)/shard_map/all_to_all | solution.py:18
  414.4 23.8 %copy.20 = bf16[8,4,128,2048]{3,2,1,0:T(8,128)(2,1)} copy(bf16[8,4,128,2048]{2,0,3,1:T(8,128)(2,1)} %bitcast.3) | data formatting | bytes 33554432 | tf_op jit(solution)/shard_map/all_to_all | solution.py:18
  438.2 18.1 %convolution_bitcast_fusion = f32[512,512]{1,0:T(8,128)} fusion(bf16[8,512,2048]{2,1,0:T(8,128)(2,1)} %bitcast.94), kind=kOutput, calls=%fused_computation.3 | convolution fusion | flops 8589934592 | bytes 17825792 | tf_op jit(solution)/shard_map/vic,vjc->ij/dot_general | solution.py:19
  457.4 9.8 custom-call.9
  467.7 81.1 %all-reduce.2.cloned.1.call-done = f32[512,512]{1,0:T(8,128)} async-done(((f32[512,512]{1,0:T(8,128)}), f32[512,512]{1,0:T(8,128)}) %all-reduce.2.cloned.1.call-update) | async-done | bytes 1048592 | tf_op jit(solution)/shard_map/psum | solution.py:20
  548.8 2.2 fusion.27
  551.8 11.7 %cholesky.100 = f32[128,128]{1,0:T(8,128)S(1)} custom-call(f32[128,128]{1,0:T(8,128)S(1)} %fusion.13), custom_call_target="Cholesky" | custom-call | tf_op jit(solution)/shard_map/jit(cholesky)/cholesky | solution.py:11
  563.5 0.7 compare_reduce_fusion.3
  564.2 0.7 fusion.2
  564.9 9.8 custom-call.10
  575.2 2.2 fusion.29
  577.4 0.8 fusion.30
  578.3 11.7 %cholesky.111 = f32[128,128]{1,0:T(8,128)S(1)} custom-call(f32[128,128]{1,0:T(8,128)S(1)} %fusion.11), custom_call_target="Cholesky" | custom-call | tf_op jit(solution)/shard_map/jit(cholesky)/cholesky | solution.py:11
  590.0 0.7 compare_reduce_fusion.2
  590.7 0.7 fusion.3
  591.5 9.8 custom-call.11
  601.7 2.2 fusion.31
  604.6 11.7 %cholesky.122 = f32[128,128]{1,0:T(8,128)S(1)} custom-call(f32[128,128]{1,0:T(8,128)S(1)} %fusion.9), custom_call_target="Cholesky" | custom-call | tf_op jit(solution)/shard_map/jit(cholesky)/cholesky | solution.py:11
  616.4 0.7 compare_reduce_fusion.1
  617.1 0.7 fusion.4
  617.8 10.0 %custom-call.12 = f32[1,128,128]{1,2,0:T(8,128)S(1)} custom-call(f32[1,128,128]{2,1,0:T(8,128)S(1)} %fusion.4), custom_call_target="InvertDiagBlocksLowerTriangular" | custom-call | tf_op jit(solution)/shard_map/triangular_solve/custom-call.0 | solution.py:12
  628.2 2.2 fusion.33
  631.2 11.7 %cholesky.133 = f32[128,128]{1,0:T(8,128)S(1)} custom-call(f32[128,128]{1,0:T(8,128)S(1)} %fusion.7), custom_call_target="Cholesky" | custom-call | tf_op jit(solution)/shard_map/jit(cholesky)/cholesky | solution.py:11
  642.9 0.7 compare_reduce_fusion
  644.3 9.8 custom-call.13
  654.7 10.4 %convolution_convert_fusion.1 = bf16[8,128,2048]{2,1,0:T(8,128)(2,1)} fusion(bf16[8,512,2048]{2,1,0:T(8,128)(2,1)} %bitcast.95, f32[8,128]{1,0:T(8,128)S(1)} %fusion.24, f32[512,128]{1,0:T(8,128)S(1)} %copy.26), kind=kOutput, calls=%fused_computation.1 | convolution fusion | flops 2150629376 | bytes 21237760 | tf_op jit(solution)/shard_map/vir,vic->vrc/dot_general | solution.py:27
  665.3 286.0 %all-gather.2.cloned.1.call-done = bf16[8,128,8192]{2,1,0:T(8,128)(2,1)} async-done(((bf16[8,128,2048]{2,1,0:T(8,128)(2,1)}), bf16[8,128,8192]{2,1,0:T(8,128)(2,1)}) %all-gather.2.cloned.1.call-update) | async-done | bytes 16777232 | tf_op jit(solution)/shard_map/all_gather | solution.py:34
  951.4 11.4 %convolution_convert_fusion = bf16[8,128,8192]{2,1,0:T(8,128)(2,1)} fusion(bf16[8,128,8192]{2,1,0:T(8,128)(2,1)} %all-gather.2.cloned.1.call-done, bf16[8,512,128]{2,1,0:T(8,128)(2,1)S(1)} %multiply_convert_fusion, s32[]{:T(128)S(6)} %select_n.6), kind=kOutput, calls=%fused_computation | convolution fusion | flops 2155872256 | bytes 33816580 | tf_op jit(solution)/shard_map/vir,vrc->vic/dot_general | solution.py:31
  962.8 15.6 %copy.30 = bf16[128,8,32,256]{3,2,1,0:T(8,128)(2,1)} copy(bf16[128,8,32,256]{3,1,2,0:T(8,128)(2,1)} %bitcast.93) | data formatting | bytes 33554432
  (38 shorter events, 8.0 us)
Async XLA Ops:
  6.5 43.3 %copy-start = (f32[512,128]{1,0:T(8,128)S(1)}, f32[512,128]{1,0:T(8,128)}, u32[]{:S(2)}) copy-start(f32[512,128]{1,0:T(8,128)} %param.8) | copy-start | bytes 786436
  42.8 371.6 %all-to-all-start = ((bf16[8,128,8192]{1,0,2:T(8,128)(2,1)}), bf16[8,128,8192]{1,0,2:T(8,128)(2,1)}, u32[]{:S(2)}, u32[]{:S(2)}) async-start(bf16[8,128,8192]{1,0,2:T(8,128)(2,1)} %bitcast.96), calls=%async_computation | async-start | bytes 33554432 | tf_op jit(solution)/shard_map/all_to_all | solution.py:18
  49.8 499.0 %all-reduce.2.cloned.1.call-start = ((), (), s32[]{:S(2)}) async-start(), calls=%async_computation.1 | async-start | bytes 2097152 | tf_op jit(solution)/shard_map/psum | solution.py:20
  438.2 29.0 %copy-start.1 = (s32[8]{0:T(128)S(1)}, s32[8]{0:T(128)}, u32[]{:S(2)}) copy-start(s32[8]{0:T(128)} %param.7) | copy-start | bytes 100
  456.3 495.0 %all-gather.2.cloned.1.call-start = ((), (), s32[]{:S(2)}) async-start(), calls=%async_computation.2 | async-start | bytes 20971520 | tf_op jit(solution)/shard_map/all_gather | solution.py:34
Sparse Core Ops, SparseCore 0:
  456.4 92.3 all-reduce.1
  665.3 286.0 all-gather.1
where the time goes:
time: 995 us; the launch traced here: 986 us
  waiting for transfers between devices  719 us (72%)
  other arithmetic  115 us (12%)
  local copies, waits for them, and re-layouts  76.3 us (8%)
  matrix products  54 us (5%)
  between operations  14.1 us (1%)
    all_to_all x1, waiting for transfers between devices, on_device(): lax.all_to_all(flat, 'fib', split_axis=2, concat_axis=1, tiled=True)  351 us
    all_gather x1, waiting for transfers between devices, on_device(): lax.all_gather(core, 'fib', axis=2, tiled=True)  286 us
    psum x1, waiting for transfers between devices, on_device(): gram = lax.psum(partial_value, ('fib', 'slab', 'var'))  81.1 us
    another operation x15, other arithmetic, orthonormal(): factor = jnp.linalg.cholesky(small)  62.2 us
    another operation x10, other arithmetic, orthonormal(): lax.linalg.triangular_solve(factor, block, left_side=False, lower=True, t...  52.6 us
    unnamed x6, local copies, waits for them, and re-layouts  51.9 us
    all_to_all x1, local copies, waits for them, and re-layouts, on_device(): lax.all_to_all(flat, 'fib', split_axis=2, concat_axis=1, tiled=True)  23.8 us
  transfers between devices with their start and end apart: 3, of which 3 were waited for; matrix products, arithmetic and copies ran while one was open for 2% of the time, Pallas kernels for 0%

commit v1 on v0

v1 whole, which is shorter than its diff:
```python
import functools

import jax
import jax.numpy as jnp
from jax import lax
from jax.experimental import pallas as pl
from jax.experimental.pallas import tpu as pltpu
from jax.sharding import PartitionSpec as P

ITERS = 4
MESH = pl.DeviceIdType.MESH
ANY = pl.BlockSpec(memory_space=pl.ANY)
VMEM = pl.BlockSpec(memory_space=pltpu.VMEM)
WINDOW = 3


def greet(axis, peers):
    barrier = pltpu.get_barrier_semaphore()
    for peer in peers:
        pl.semaphore_signal(barrier, inc=1, device_id={axis: peer}, device_id_type=MESH)
    pl.semaphore_wait(barrier, len(peers))


def exchange_kernel(n, flat, fibres, gram, held, send_sem, recv_sem, own_sem, load_sem):
    nvars, rows, _ = flat.shape
    share = fibres.shape[2]
    tile = min(share, 512)
    me = lax.axis_index("fib")
    greet("fib", [lax.rem(me + off, n) for off in range(1, n)])
    gram[...] = jnp.zeros_like(gram)

    def place(who, length):
        return pl.ds(pl.multiple_of(who * length, length), length)

    def remote(v, off):
        peer = lax.rem(me + off, n)
        return pltpu.make_async_remote_copy(
            src_ref=flat.at[v, :, place(peer, share)],
            dst_ref=fibres.at[v, place(me, rows), :],
            send_sem=send_sem.at[v, off],
            recv_sem=recv_sem.at[v, off],
            device_id={"fib": peer},
            device_id_type=MESH,
        )

    def arrival(v, off):
        source = lax.rem(me + n - off, n)
        return pltpu.make_async_remote_copy(
            src_ref=flat.at[v, :, place(me, share)],
            dst_ref=fibres.at[v, place(source, rows), :],
            send_sem=send_sem.at[v, off],
            recv_sem=recv_sem.at[v, off],
            device_id={"fib": lax.rem(me + off, n)},
            device_id_type=MESH,
        )

    def own(v):
        return pltpu.make_async_copy(
            flat.at[v, :, place(me, share)], fibres.at[v, place(me, rows), :], own_sem.at[v]
        )

    def start(v):
        own(v).start()
        pl.loop(1, n)(lambda off: remote(v, off).start())

    def finish(v):
        own(v).wait()

        @pl.loop(1, n)
        def _(off):
            remote(v, off).wait_send()
            arrival(v, off).wait_recv()

        load = pltpu.make_async_copy(fibres.at[v], held, load_sem)
        load.start()
        load.wait()

        @pl.loop(0, share // tile)
        def _(t):
            block = held[:, pl.ds(pl.multiple_of(t * tile, tile), tile)]
            gram[...] += lax.dot_general(
                block, block, (((1,), (1,)), ((), ())), preferred_element_type=jnp.float32
            )

    @pl.loop(0, nvars + WINDOW)
    def _(step):
        pl.when(step < nvars)(lambda: start(step))
        pl.when(step >= WINDOW)(lambda: finish(step - WINDOW))


def exchange(flat, n):
    nvars, rows, columns = flat.shape
    whole, share = rows * n, columns // n
    return pl.pallas_call(
        functools.partial(exchange_kernel, n),
        out_shape=(
            jax.ShapeDtypeStruct((nvars, whole, share), flat.dtype),
            jax.ShapeDtypeStruct((whole, whole), jnp.float32),
        ),
        in_specs=[ANY],
        out_specs=(ANY, VMEM),
        scratch_shapes=[
            pltpu.VMEM((whole, share), flat.dtype),
            pltpu.SemaphoreType.DMA((nvars, n)),
            pltpu.SemaphoreType.DMA((nvars, n)),
            pltpu.SemaphoreType.DMA((nvars,)),
            pltpu.SemaphoreType.DMA,
        ],
        compiler_params=pltpu.CompilerParams(
            collective_id=0, has_side_effects=True, vmem_limit_bytes=32 * 2**20
        ),
        name="exchange",
    )(flat)


def reduce_kernel(axes, part, total, held, *scratch):
    lands, sems = scratch[: len(axes)], scratch[len(axes):]
    barrier = pltpu.get_barrier_semaphore()
    count = 0
    for axis, n in axes:
        me = lax.axis_index(axis)
        for off in range(1, n):
            pl.semaphore_signal(
                barrier, inc=1, device_id={axis: lax.rem(me + off, n)}, device_id_type=MESH
            )
            count += 1
    pl.semaphore_wait(barrier, count)
    base, length = 0, total.shape[0]
    levels = []
    for level, (axis, n) in enumerate(axes):
        me = lax.axis_index(axis)
        size = length // n
        levels.append((axis, n, me, base, size))
        source = held if level else part
        copies = []
        for off in range(1, n):
            peer = lax.rem(me + off, n)
            copies.append(
                pltpu.make_async_remote_copy(
                    src_ref=source.at[pl.ds(pl.multiple_of(base + peer * size, size), size), :],
                    dst_ref=lands[level].at[off - 1],
                    send_sem=sems[0].at[level, off],
                    recv_sem=sems[1].at[level, off],
                    device_id={axis: peer},
                    device_id_type=MESH,
                )
            )
            copies[-1].start()
        base = base + me * size
        length = size
        for copy in copies:
            copy.wait()
        mine = pl.ds(pl.multiple_of(base, size), size)
        value = source[mine, :]
        for off in range(1, n):
            value += lands[level][off - 1]
        target = held if level < len(axes) - 1 else total
        target[mine, :] = value
    for level in reversed(range(len(axes))):
        axis, n, me, start, size = levels[level]
        mine = pl.ds(pl.multiple_of(start + me * size, size), size)
        sends = []
        for off in range(1, n):
            peer = lax.rem(me + off, n)
            sends.append(
                pltpu.make_async_remote_copy(
                    src_ref=total.at[mine, :],
                    dst_ref=total.at[mine, :],
                    send_sem=sems[2].at[level, off],
                    recv_sem=sems[3].at[level, off],
                    device_id={axis: peer},
                    device_id_type=MESH,
                )
            )
            sends[-1].start()
        for off in range(1, n):
            source = lax.rem(me + n - off, n)
            theirs = pl.ds(pl.multiple_of(start + source * size, size), size)
            sends[off - 1].wait_send()
            pltpu.make_async_remote_copy(
                src_ref=total.at[mine, :],
                dst_ref=total.at[theirs, :],
                send_sem=sems[2].at[level, off],
                recv_sem=sems[3].at[level, off],
                device_id={axis: lax.rem(me + off, n)},
                device_id_type=MESH,
            ).wait_recv()


def reduce_all(part, axes):
    rows, columns = part.shape
    total = 1
    for _, n in axes:
        total *= n
    if rows % (8 * total):
        return lax.psum(part, tuple(axis for axis, _ in axes))
    lands, size = [], rows
    for _, n in axes:
        size //= n
        lands.append(pltpu.VMEM((n - 1, size, columns), jnp.float32))
    sem = pltpu.SemaphoreType.DMA((len(axes), max(n for _, n in axes)))
    return pl.pallas_call(
        functools.partial(reduce_kernel, axes),
        out_shape=jax.ShapeDtypeStruct(part.shape, part.dtype),
        in_specs=[VMEM],
        out_specs=VMEM,
        scratch_shapes=[pltpu.VMEM(part.shape, jnp.float32)] + lands + [sem] * 4,
        compiler_params=pltpu.CompilerParams(
            collective_id=1, has_side_effects=True, vmem_limit_bytes=32 * 2**20
        ),
        name="reduce_all",
    )(part)


def rebuild_kernel(n, core, left_factor, out, full, stage, send_sem, recv_sem, own_sem, out_sem):
    nvars, depth, share = core.shape
    rows = left_factor.shape[1]
    me = lax.axis_index("fib")
    barrier = pltpu.get_barrier_semaphore()
    has_left, has_right = me > 0, me < n - 1
    lo, hi = me - 1, me + 1

    for flag, peer in ((has_left, lo), (has_right, hi)):

        @pl.when(flag)
        def _():
            pl.semaphore_signal(barrier, inc=1, device_id={"fib": peer}, device_id_type=MESH)

    inner = has_left & has_right
    pl.when(inner)(lambda: pl.semaphore_wait(barrier, 2))
    pl.when(jnp.logical_not(inner))(lambda: pl.semaphore_wait(barrier, 1))

    def columns(who):
        return pl.ds(pl.multiple_of(who * share, share), share)

    def copy(v, who, side, peer):
        piece = full.at[v, :, columns(who)]
        return pltpu.make_async_remote_copy(
            src_ref=piece,
            dst_ref=piece,
            send_sem=send_sem.at[side, v, who],
            recv_sem=recv_sem.at[v, who],
            device_id={"fib": peer},
            device_id_type=MESH,
        )

    def fetch(v):
        return pltpu.make_async_copy(core.at[v], full.at[v, :, columns(me)], own_sem.at[v])

    def to_right(v, who):
        return copy(v, who, 1, hi)

    def to_left(v, who):
        return copy(v, who, 0, lo)

    def write(slot, v, who):
        return pltpu.make_async_copy(
            stage.at[slot], out.at[v, :, columns(who)], out_sem.at[slot]
        )

    def rebuild(slot, v, who, first):
        pl.when(jnp.logical_not(first))(lambda: write(slot, v, who).wait())
        tile = min(share, 512)

        @pl.loop(0, share // tile)
        def _(t):
            at = pl.ds(pl.multiple_of(t * tile, tile), tile)
            source = pl.ds(pl.multiple_of(who * share + t * tile, tile), tile)
            stage[slot, :, at] = jnp.dot(
                left_factor[v], full[v, :, source], preferred_element_type=jnp.float32
            ).astype(stage.dtype)

        write(slot, v, who).start()

    pl.loop(0, nvars)(lambda v: fetch(v).start())

    @pl.loop(0, nvars)
    def _(v):
        fetch(v).wait()
        pl.when(has_left)(lambda: to_left(v, me).start())
        pl.when(has_right)(lambda: to_right(v, me).start())

    pl.loop(0, nvars)(lambda v: rebuild(2, v, me, v == 0))
    write(2, 0, me).wait()

    for hop in range(1, n):
        from_left, from_right = me - hop, me + hop
        left_ok, right_ok = from_left >= 0, from_right < n

        @pl.loop(0, nvars)
        def _(v):
            @pl.when(left_ok)
            def _():
                to_right(v, from_left).wait_recv()
                pl.when(has_right)(lambda: to_right(v, from_left).start())

            @pl.when(right_ok)
            def _():
                to_left(v, from_right).wait_recv()
                pl.when(has_left)(lambda: to_left(v, from_right).start())

            pl.when(left_ok)(lambda: rebuild(0, v, from_left, v == 0))
            pl.when(right_ok)(lambda: rebuild(1, v, from_right, v == 0))

        pl.when(left_ok)(lambda: write(0, 0, from_left).wait())
        pl.when(right_ok)(lambda: write(1, 0, from_right).wait())

    for hop in range(n):
        from_left, from_right = me - hop, me + hop

        @pl.loop(0, nvars)
        def _(v):
            pl.when((from_left >= 0) & has_right)(lambda: to_right(v, from_left).wait_send())
            pl.when((from_right < n) & has_left)(lambda: to_left(v, from_right).wait_send())


def rebuild_all(core, left_factor, n):
    nvars, depth, share = core.shape
    rows = left_factor.shape[1]
    return pl.pallas_call(
        functools.partial(rebuild_kernel, n),
        out_shape=jax.ShapeDtypeStruct((nvars, rows, share * n), core.dtype),
        in_specs=[ANY, VMEM],
        out_specs=ANY,
        scratch_shapes=[
            pltpu.VMEM((nvars, depth, share * n), core.dtype),
            pltpu.VMEM((3, rows, share), core.dtype),
            pltpu.SemaphoreType.DMA((2, nvars, n)),
            pltpu.SemaphoreType.DMA((nvars, n)),
            pltpu.SemaphoreType.DMA((nvars,)),
            pltpu.SemaphoreType.DMA((3,)),
        ],
        compiler_params=pltpu.CompilerParams(
            collective_id=2, has_side_effects=True, vmem_limit_bytes=48 * 2**20
        ),
        name="rebuild_all",
    )(core, left_factor)


def orthonormal(block):
    small = jnp.dot(block.T, block, precision=lax.Precision.HIGHEST)
    factor = jnp.linalg.cholesky(small)
    return lax.linalg.triangular_solve(factor, block, left_side=False, lower=True, transpose_a=True)


def on_device(sizes, field, rank, start_basis):
    nvars, rows, depth, width = field.shape
    n = sizes["fib"]
    flat = field.reshape(nvars, rows, depth * width)
    fibres, partial_gram = exchange(flat, n)
    gram = reduce_all(partial_gram, tuple((axis, sizes[axis]) for axis in ("var", "slab", "fib")))
    basis = orthonormal(start_basis)
    for step in range(ITERS):
        basis = orthonormal(jnp.dot(gram, basis, precision=lax.Precision.HIGHEST))
    columns = jnp.arange(basis.shape[1], dtype=jnp.int32)
    keep = (columns[None, :] < rank[:, None]).astype(basis.dtype)
    basis_bf = (basis[None, :, :] * keep[:, None, :]).astype(jnp.bfloat16)
    core = jnp.einsum("vir,vic->vrc", basis_bf, fibres, preferred_element_type=jnp.float32).astype(
        jnp.bfloat16
    )
    own_rows = lax.dynamic_slice_in_dim(basis_bf, lax.axis_index("fib") * rows, rows, 1)
    result = rebuild_all(core, own_rows, n)
    return result.reshape(nvars, rows, depth, width)


def solution(mesh):
    return jax.shard_map(
        functools.partial(on_device, dict(mesh.shape)),
        mesh=mesh,
        in_specs=(P(("grp", "var"), "fib", "slab", None), P(("grp", "var")), P()),
        out_specs=P(("grp", "var"), "fib", "slab", None),
        check_vma=False,
    )
```

time: 995 us -> 872 us (0.88)
  waiting for transfers between devices: 719 us -> 0 us
  Pallas kernels: 0 us -> 677 us
  matrix products: 54 us -> 19 us
  local copies, waits for them, and re-layouts: 76.3 us -> 50.2 us
  between operations: 14.1 us -> 0.57 us
    pallas_call x0 -> x3, Pallas kernels: none -> 677 us  [the longest x1 358 us: exchange(): pl.pallas_call(functools.partial(exchange_kernel, n), out_shape=(jax.Shap...]
    all_to_all x1 -> x0, waiting for transfers between devices: 351 us -> none  [on_device(): lax.all_to_all(flat, 'fib', split_axis=2, concat_axis=1, tiled=True)]
    all_gather x1 -> x0, waiting for transfers between devices: 286 us -> none  [on_device(): lax.all_gather(core, 'fib', axis=2, tiled=True)]
    psum x1 -> x0, waiting for transfers between devices: 81.1 us -> none  [on_device(): gram = lax.psum(partial_value, ('fib', 'slab', 'var'))]
    dot_general x2 -> x0, matrix products: 29.5 us -> none  [the longest x1 18.1 us: on_device(): jnp.einsum('vic,vjc->ij', fibres, fibres, preferred_element_type=jnp.floa...]
    unnamed x6 -> x11, local copies, waits for them, and re-layouts: 51.9 us -> 24 us
    reshape x0 -> x1, local copies, waits for them, and re-layouts: none -> 25.6 us  [on_device(): flat = field.reshape(nvars, rows, depth * width)]
    all_to_all x1 -> x0, local copies, waits for them, and re-layouts: 23.8 us -> none  [on_device(): lax.all_to_all(flat, 'fib', split_axis=2, concat_axis=1, tiled=True)]
  transfers between devices with their start and end apart: 3 -> 0, of which waited for: 3 -> 0; matrix products, arithmetic and copies ran while one was open for 2% -> 0% of each run, Pallas kernels for 0% -> 0%
where the time goes in v1:
time: 872 us; the launch traced here: 862 us
  Pallas kernels  677 us (78%)
  other arithmetic  116 us (13%)
  local copies, waits for them, and re-layouts  50.2 us (6%)
  matrix products  19 us (2%)
    pallas_call x1, Pallas kernels, exchange(): pl.pallas_call(functools.partial(exchange_kernel, n), out_shape=(jax.Shap...  358 us
    pallas_call x1, Pallas kernels, rebuild_all(): pl.pallas_call(functools.partial(rebuild_kernel, n), out_shape=jax.ShapeD...  277 us
    another operation x15, other arithmetic, orthonormal(): factor = jnp.linalg.cholesky(small)  62.8 us
    another operation x10, other arithmetic, orthonormal(): lax.linalg.triangular_solve(factor, block, left_side=False, lower=True, t...  52.7 us
    pallas_call x1, Pallas kernels, reduce_all(): pl.pallas_call(functools.partial(reduce_kernel, axes), out_shape=jax.Shap...  41.9 us
    reshape x1, local copies, waits for them, and re-layouts, on_device(): flat = field.reshape(nvars, rows, depth * width)  25.6 us
    unnamed x11, local copies, waits for them, and re-layouts  24 us

profile of v1, /device:TPU:0, one launch (start us, length us, event | category | flops | bytes accessed | tf_op | source)
XLA Modules:
  0.0 862.2 jit_solution(13529781347346082292)
XLA Ops:
  0.0 25.6 %reshape.36.flat = bf16[8,128,8192]{2,1,0:T(8,128)(2,1)} reshape(bf16[8,128,32,256]{3,2,1,0:T(8,128)(2,1)} %param.6) | data formatting | bytes 33554432 | tf_op jit(solution)/shard_map/reshape | solution.py:349
  25.6 357.5 %exchange.1 = (bf16[8,512,2048]{2,1,0:T(8,128)(2,1)S(1)}, f32[512,512]{1,0:T(8,128)S(1)}) custom-call(bf16[8,128,8192]{2,1,0:T(8,128)(2,1)} %reshape.36.flat), custom_call_target="tpu_custom_call" | custom-call | tf_op jit(solution)/shard_map/exchange/pallas_call | solution.py:94
  383.1 6.2 copy-done.2
  390.1 11.7 %cholesky.89 = f32[128,128]{1,0:T(8,128)S(1)} custom-call(f32[128,128]{1,0:T(8,128)S(1)} %fusion.18), custom_call_target="Cholesky" | custom-call | tf_op jit(solution)/shard_map/jit(cholesky)/cholesky | solution.py:342
  401.8 0.7 compare_reduce_fusion.4
  402.5 0.7 fusion.4
  403.3 9.8 %custom-call.9 = f32[1,128,128]{1,2,0:T(8,128)S(1)} custom-call(f32[1,128,128]{2,1,0:T(8,128)S(1)} %fusion.4), custom_call_target="InvertDiagBlocksLowerTriangular" | custom-call | tf_op jit(solution)/shard_map/triangular_solve/custom-call.0 | solution.py:343
  413.5 41.9 %reduce_all.1 = f32[512,512]{1,0:T(8,128)S(1)} custom-call(f32[512,512]{1,0:T(8,128)S(1)} %get-tuple-element.9.part), custom_call_target="tpu_custom_call" | custom-call | tf_op jit(solution)/shard_map/reduce_all/pallas_call | solution.py:202
  455.4 1.2 fusion.29
  457.1 12.0 %cholesky.100 = f32[128,128]{1,0:T(8,128)S(1)} custom-call(f32[128,128]{1,0:T(8,128)S(1)} %fusion.16), custom_call_target="Cholesky" | custom-call | tf_op jit(solution)/shard_map/jit(cholesky)/cholesky | solution.py:342
  469.2 0.7 compare_reduce_fusion.3
  469.9 0.7 fusion.5
  470.6 9.8 %custom-call.10 = f32[1,128,128]{1,2,0:T(8,128)S(1)} custom-call(f32[1,128,128]{2,1,0:T(8,128)S(1)} %fusion.5), custom_call_target="InvertDiagBlocksLowerTriangular" | custom-call | tf_op jit(solution)/shard_map/triangular_solve/custom-call.0 | solution.py:343
  480.8 1.2 fusion.31
  482.5 11.7 %cholesky.111 = f32[128,128]{1,0:T(8,128)S(1)} custom-call(f32[128,128]{1,0:T(8,128)S(1)} %fusion.14), custom_call_target="Cholesky" | custom-call | tf_op jit(solution)/shard_map/jit(cholesky)/cholesky | solution.py:342
  494.3 0.7 compare_reduce_fusion.2
  495.0 0.7 fusion.6
  495.7 9.8 %custom-call.11 = f32[1,128,128]{1,2,0:T(8,128)S(1)} custom-call(f32[1,128,128]{2,1,0:T(8,128)S(1)} %fusion.6), custom_call_target="InvertDiagBlocksLowerTriangular" | custom-call | tf_op jit(solution)/shard_map/triangular_solve/custom-call.0 | solution.py:343
  505.9 1.2 fusion.33
  507.6 11.9 %cholesky.122 = f32[128,128]{1,0:T(8,128)S(1)} custom-call(f32[128,128]{1,0:T(8,128)S(1)} %fusion.12), custom_call_target="Cholesky" | custom-call | tf_op jit(solution)/shard_map/jit(cholesky)/cholesky | solution.py:342
  519.5 0.7 compare_reduce_fusion.1
  520.2 0.7 fusion.7
  521.0 9.8 %custom-call.12 = f32[1,128,128]{1,2,0:T(8,128)S(1)} custom-call(f32[1,128,128]{2,1,0:T(8,128)S(1)} %fusion.7), custom_call_target="InvertDiagBlocksLowerTriangular" | custom-call | tf_op jit(solution)/shard_map/triangular_solve/custom-call.0 | solution.py:343
  531.2 1.2 fusion.35
  532.9 11.7 %cholesky.133 = f32[128,128]{1,0:T(8,128)S(1)} custom-call(f32[128,128]{1,0:T(8,128)S(1)} %fusion.10), custom_call_target="Cholesky" | custom-call | tf_op jit(solution)/shard_map/jit(cholesky)/cholesky | solution.py:342
  544.6 0.7 compare_reduce_fusion
  545.4 0.7 fusion.8
  546.1 10.0 %custom-call.13 = f32[1,128,128]{1,2,0:T(8,128)S(1)} custom-call(f32[1,128,128]{2,1,0:T(8,128)S(1)} %fusion.8), custom_call_target="InvertDiagBlocksLowerTriangular" | custom-call | tf_op jit(solution)/shard_map/triangular_solve/custom-call.0 | solution.py:343
  556.6 10.1 %convolution_convert_fusion.core = bf16[8,128,2048]{2,1,0:T(8,128)(2,1)} fusion(bf16[8,512,2048]{2,1,0:T(8,128)(2,1)} %copy-done.2, f32[8,128]{1,0:T(8,128)S(1)} %fusion.27, f32[512,128]{1,0:T(8,128)S(1)} %copy.9), kind=kOutput, calls=%fused_computation | convolution fusion | flops 2150629376 | bytes 21237760 | tf_op jit(solution)/shard_map/vir,vic->vrc/dot_general | solution.py:358
  567.0 2.2 copy-done.3
  569.2 277.1 %rebuild_all.1 = bf16[8,128,8192]{2,1,0:T(8,128)(2,1)} custom-call(bf16[8,128,2048]{2,1,0:T(8,128)(2,1)S(1)} %copy-done.3, bf16[8,128,128]{2,1,0:T(8,128)(2,1)S(1)} %constant_dynamic-slice_fusion.left_factor), custom_call_target="tpu_custom_call" | custom-call | tf_op jit(solution)/shard_map/rebuild_all/pallas_call | solution.py:320
  846.3 15.7 %copy.12 = bf16[128,8,32,256]{3,2,1,0:T(8,128)(2,1)} copy(bf16[128,8,32,256]{3,1,2,0:T(8,128)(2,1)} %bitcast.93) | data formatting | bytes 33554432
  (37 shorter events, 5.3 us)
Async XLA Ops:
  0.0 389.4 %copy-start = (f32[512,128]{1,0:T(8,128)S(1)}, f32[512,128]{1,0:T(8,128)}, u32[]{:S(2)}) copy-start(f32[512,128]{1,0:T(8,128)} %param.8) | copy-start | bytes 786436
  25.6 363.7 %copy-start.4 = (s32[8]{0:T(128)S(1)}, s32[8]{0:T(128)}, u32[]{:S(2)}) copy-start(s32[8]{0:T(128)} %param.7) | copy-start | bytes 100
  383.1 6.2 copy-start.2
  567.0 2.2 copy-start.3
  846.3 15.7 %copy-start.1 = (f32[512,128]{1,0:T(8,128)S(1)}, f32[512,128]{1,0:T(8,128)}, u32[]{:S(2)}) copy-start(f32[512,128]{1,0:T(8,128)} %param.8) | copy-start | bytes 786436

commit v2 on v1

--- a/solution.py
+++ b/solution.py
@@ -337,10 +337,65 @@
     )(core, left_factor)
 
 
+def highest(a, b, dims):
+    return lax.dot_general(
+        a,
+        b,
+        ((dims[:1], dims[1:]), ((), ())),
+        precision=lax.Precision.HIGHEST,
+        preferred_element_type=jnp.float32,
+    )
+
+
+def eliminate(block):
+    size = block.shape[0]
+    row = lax.broadcasted_iota(jnp.int32, block.shape, 0)
+    scale = jnp.zeros_like(block)
+    for j in range(size):
+        column = jnp.broadcast_to(block[:, j:j + 1], block.shape)
+        pivot = column[j:j + 1, :]
+        scale = jnp.where(row == j, pivot, scale)
+        if j < size - 1:
+            step = column * (block[j:j + 1, :] / pivot)
+            block = jnp.where(row > j, block - step, block)
+    return block * lax.rsqrt(scale)
+
+
 def orthonormal(block):
-    small = jnp.dot(block.T, block, precision=lax.Precision.HIGHEST)
-    factor = jnp.linalg.cholesky(small)
-    return lax.linalg.triangular_solve(factor, block, left_side=False, lower=True, transpose_a=True)
+    size, nb = block.shape[1], 16
+    small = highest(block, block, (0, 0))
+    at = lax.broadcasted_iota(jnp.int32, (size, size), 0)
+    to = lax.broadcasted_iota(jnp.int32, (size, size), 1)
+    eye = (at == to).astype(jnp.float32)
+    work = jnp.concatenate([small, eye], axis=1)
+    inverse = []
+    for k in range(0, size, nb):
+        rows = work[k:k + nb, :]
+        solved = eliminate(jnp.concatenate([rows[:, k:k + nb], eye[:nb, :nb]], axis=1))[:, nb:]
+        panel = highest(solved, rows, (1, 0))
+        inverse.append(panel[:, size:])
+        if k + nb < size:
+            work = work - highest(panel[:, :size], panel, (0, 0))
+    return highest(block, jnp.concatenate(inverse, axis=0), (1, 1))
+
+
+def iterate_kernel(gram, start, basis):
+    basis[...] = orthonormal(start[...])
+
+    @pl.loop(0, ITERS)
+    def _(step):
+        basis[...] = orthonormal(highest(gram[...], basis[...], (1, 0)))
+
+
+def iterate(gram, start):
+    return pl.pallas_call(
+        iterate_kernel,
+        out_shape=jax.ShapeDtypeStruct(start.shape, jnp.float32),
+        in_specs=[VMEM, VMEM],
+        out_specs=VMEM,
+        compiler_params=pltpu.CompilerParams(vmem_limit_bytes=32 * 2**20),
+        name="iterate",
+    )(gram, start)
 
 
 def on_device(sizes, field, rank, start_basis):
@@ -349,9 +404,7 @@
     flat = field.reshape(nvars, rows, depth * width)
     fibres, partial_gram = exchange(flat, n)
     gram = reduce_all(partial_gram, tuple((axis, sizes[axis]) for axis in ("var", "slab", "fib")))
-    basis = orthonormal(start_basis)
-    for step in range(ITERS):
-        basis = orthonormal(jnp.dot(gram, basis, precision=lax.Precision.HIGHEST))
+    basis = iterate(gram, start_basis)
     columns = jnp.arange(basis.shape[1], dtype=jnp.int32)
     keep = (columns[None, :] < rank[:, None]).astype(basis.dtype)
     basis_bf = (basis[None, :, :] * keep[:, None, :]).astype(jnp.bfloat16)

time: 872 us -> 826 us (0.947)
  other arithmetic: 116 us -> 0.24 us
  Pallas kernels: 677 us -> 764 us
  matrix products: 19 us -> 10.2 us
    another operation x25 -> x0, other arithmetic: 116 us -> none  [the longest x15 62.8 us: orthonormal(): factor = jnp.linalg.cholesky(small)]
    pallas_call x0 -> x1, Pallas kernels: none -> 87.9 us  [iterate(): pl.pallas_call(iterate_kernel, out_shape=jax.ShapeDtypeStruct(start.shape...]
    unnamed x11 -> x9, local copies, waits for them, and re-layouts: 24 us -> 24 us
where the time goes in v2:
time: 826 us; the launch traced here: 825 us
  Pallas kernels  764 us (92%)
  local copies, waits for them, and re-layouts  49.5 us (6%)
  matrix products  10.2 us (1%)
    pallas_call x1, Pallas kernels, exchange(): pl.pallas_call(functools.partial(exchange_kernel, n), out_shape=(jax.Shap...  358 us
    pallas_call x1, Pallas kernels, rebuild_all(): pl.pallas_call(functools.partial(rebuild_kernel, n), out_shape=jax.ShapeD...  277 us
    pallas_call x1, Pallas kernels, iterate(): pl.pallas_call(iterate_kernel, out_shape=jax.ShapeDtypeStruct(start.shape...  87.9 us
    pallas_call x1, Pallas kernels, reduce_all(): pl.pallas_call(functools.partial(reduce_kernel, axes), out_shape=jax.Shap...  41.8 us
    reshape x1, local copies, waits for them, and re-layouts, on_device(): flat = field.reshape(nvars, rows, depth * width)  25.5 us
    unnamed x9, local copies, waits for them, and re-layouts  24 us

profile of v2, /device:TPU:0, one launch (start us, length us, event | category | flops | bytes accessed | tf_op | source)
XLA Modules:
  0.0 824.6 jit_solution(2811042772725935945)
XLA Ops:
  0.0 25.5 %reshape.25.flat = bf16[8,128,8192]{2,1,0:T(8,128)(2,1)} reshape(bf16[8,128,32,256]{3,2,1,0:T(8,128)(2,1)} %param.3) | data formatting | bytes 33554432 | tf_op jit(solution)/shard_map/reshape | solution.py:404
  25.5 0.0 copy-start.3
  25.5 0.0 copy-start.2
  25.5 357.5 %exchange.1 = (bf16[8,512,2048]{2,1,0:T(8,128)(2,1)S(1)}, f32[512,512]{1,0:T(8,128)S(1)}) custom-call(bf16[8,128,8192]{2,1,0:T(8,128)(2,1)} %reshape.25.flat), custom_call_target="tpu_custom_call" | custom-call | tf_op jit(solution)/shard_map/exchange/pallas_call | solution.py:94
  383.1 0.0 copy-start
  383.1 6.2 copy-done
  389.2 0.0 copy-done.3
  389.2 0.1 fusion
  389.3 41.8 %reduce_all.1.gram = f32[512,512]{1,0:T(8,128)S(1)} custom-call(f32[512,512]{1,0:T(8,128)S(1)} %get-tuple-element.7.part), custom_call_target="tpu_custom_call" | custom-call | tf_op jit(solution)/shard_map/reduce_all/pallas_call | solution.py:202
  431.2 0.0 copy-done.2
  431.2 87.9 %iterate.1 = f32[512,128]{1,0:T(8,128)S(1)} custom-call(f32[512,512]{1,0:T(8,128)S(1)} %reduce_all.1.gram, f32[512,128]{1,0:T(8,128)S(1)} %copy-done.2), custom_call_target="tpu_custom_call" | custom-call | tf_op jit(solution)/shard_map/iterate/pallas_call | solution.py:391
  519.1 10.2 %convolution_convert_fusion.core = bf16[8,128,2048]{2,1,0:T(8,128)(2,1)} fusion(bf16[8,512,2048]{2,1,0:T(8,128)(2,1)} %copy-done, f32[8,128]{1,0:T(8,128)S(1)} %fusion, f32[512,128]{1,0:T(8,128)S(1)} %iterate.1), kind=kOutput, calls=%fused_computation | convolution fusion | flops 2150629376 | bytes 21237760 | tf_op jit(solution)/shard_map/vir,vic->vrc/dot_general | solution.py:411
  529.4 0.2 multiply_convert_fusion
  529.6 0.0 copy-start.1
  529.6 2.2 copy-done.1
  531.8 277.2 %rebuild_all.1 = bf16[8,128,8192]{2,1,0:T(8,128)(2,1)} custom-call(bf16[8,128,2048]{2,1,0:T(8,128)(2,1)S(1)} %copy-done.1, bf16[8,128,128]{2,1,0:T(8,128)(2,1)S(1)} %constant_dynamic-slice_fusion.left_factor), custom_call_target="tpu_custom_call" | custom-call | tf_op jit(solution)/shard_map/rebuild_all/pallas_call | solution.py:320
  809.0 15.6 %copy.6 = bf16[128,8,32,256]{3,2,1,0:T(8,128)(2,1)} copy(bf16[128,8,32,256]{3,1,2,0:T(8,128)(2,1)} %bitcast.7) | data formatting | bytes 33554432
  (1 shorter events, 0.0 us)
Async XLA Ops:
  25.5 363.7 %copy-start.3 = (s32[8]{0:T(128)S(1)}, s32[8]{0:T(128)}, u32[]{:S(2)}) copy-start(s32[8]{0:T(128)} %param.4) | copy-start | bytes 100
  25.5 405.6 %copy-start.2 = (f32[512,128]{1,0:T(8,128)S(1)}, f32[512,128]{1,0:T(8,128)}, u32[]{:S(2)}) copy-start(f32[512,128]{1,0:T(8,128)} %start.1) | copy-start | bytes 786436
  383.1 6.2 copy-start
  529.6 2.2 copy-start.1

commit v3 on v2

--- a/solution.py
+++ b/solution.py
@@ -12,6 +12,8 @@
 ANY = pl.BlockSpec(memory_space=pl.ANY)
 VMEM = pl.BlockSpec(memory_space=pltpu.VMEM)
 WINDOW = 3
+CHUNK = 64
+PARTS = (6, 8, 9, 10, 11, 12, 13, 14, 16)
 
 
 def greet(axis, peers):
@@ -21,7 +23,7 @@
     pl.semaphore_wait(barrier, len(peers))
 
 
-def exchange_kernel(n, flat, fibres, gram, held, send_sem, recv_sem, own_sem, load_sem):
+def exchange_kernel(n, flat, start_basis, fibres, gram, basis, held, send_sem, recv_sem, own_sem, load_sem):
     nvars, rows, _ = flat.shape
     share = fibres.shape[2]
     tile = min(share, 512)
@@ -82,13 +84,17 @@
                 block, block, (((1,), (1,)), ((), ())), preferred_element_type=jnp.float32
             )
 
-    @pl.loop(0, nvars + WINDOW)
+    first = min(WINDOW, nvars)
+    pl.loop(0, first)(start)
+    basis[...] = orthonormal(start_basis[...])
+
+    @pl.loop(first, nvars + WINDOW)
     def _(step):
         pl.when(step < nvars)(lambda: start(step))
         pl.when(step >= WINDOW)(lambda: finish(step - WINDOW))
 
 
-def exchange(flat, n):
+def exchange(flat, start_basis, n):
     nvars, rows, columns = flat.shape
     whole, share = rows * n, columns // n
     return pl.pallas_call(
@@ -96,9 +102,10 @@
         out_shape=(
             jax.ShapeDtypeStruct((nvars, whole, share), flat.dtype),
             jax.ShapeDtypeStruct((whole, whole), jnp.float32),
+            jax.ShapeDtypeStruct(start_basis.shape, jnp.float32),
         ),
-        in_specs=[ANY],
-        out_specs=(ANY, VMEM),
+        in_specs=[ANY, VMEM],
+        out_specs=(ANY, VMEM, VMEM),
         scratch_shapes=[
             pltpu.VMEM((whole, share), flat.dtype),
             pltpu.SemaphoreType.DMA((nvars, n)),
@@ -110,7 +117,7 @@
             collective_id=0, has_side_effects=True, vmem_limit_bytes=32 * 2**20
         ),
         name="exchange",
-    )(flat)
+    )(flat, start_basis)
 
 
 def reduce_kernel(axes, part, total, held, *scratch):
@@ -213,8 +220,9 @@
 
 
 def rebuild_kernel(n, core, left_factor, out, full, stage, send_sem, recv_sem, own_sem, out_sem):
-    nvars, depth, share = core.shape
-    rows = left_factor.shape[1]
+    packed, share = core.shape
+    chunks = packed // CHUNK
+    tile = min(share, 512)
     me = lax.axis_index("fib")
     barrier = pltpu.get_barrier_semaphore()
     has_left, has_right = me > 0, me < n - 1
@@ -233,108 +241,132 @@
     def columns(who):
         return pl.ds(pl.multiple_of(who * share, share), share)
 
-    def copy(v, who, side, peer):
-        piece = full.at[v, :, columns(who)]
+    def rows(c):
+        return pl.ds(pl.multiple_of(c * CHUNK, CHUNK), CHUNK)
+
+    def copy(c, who, side, peer):
+        piece = full.at[rows(c), columns(who)]
         return pltpu.make_async_remote_copy(
             src_ref=piece,
             dst_ref=piece,
-            send_sem=send_sem.at[side, v, who],
-            recv_sem=recv_sem.at[v, who],
+            send_sem=send_sem.at[side, c, who],
+            recv_sem=recv_sem.at[c, who],
             device_id={"fib": peer},
             device_id_type=MESH,
         )
 
-    def fetch(v):
-        return pltpu.make_async_copy(core.at[v], full.at[v, :, columns(me)], own_sem.at[v])
-
-    def to_right(v, who):
-        return copy(v, who, 1, hi)
-
-    def to_left(v, who):
-        return copy(v, who, 0, lo)
-
-    def write(slot, v, who):
+    def fetch(c):
         return pltpu.make_async_copy(
-            stage.at[slot], out.at[v, :, columns(who)], out_sem.at[slot]
+            core.at[rows(c), :], full.at[rows(c), columns(me)], own_sem.at[c]
         )
 
-    def rebuild(slot, v, who, first):
-        pl.when(jnp.logical_not(first))(lambda: write(slot, v, who).wait())
-        tile = min(share, 512)
-
+    def to_right(c, who):
+        return copy(c, who, 1, hi)
+
+    def to_left(c, who):
+        return copy(c, who, 0, lo)
+
+    def write(slot, who):
+        return pltpu.make_async_copy(stage.at[slot], out.at[:, columns(who)], out_sem.at[slot])
+
+    def rebuild(slot, who):
         @pl.loop(0, share // tile)
         def _(t):
             at = pl.ds(pl.multiple_of(t * tile, tile), tile)
             source = pl.ds(pl.multiple_of(who * share + t * tile, tile), tile)
             stage[slot, :, at] = jnp.dot(
-                left_factor[v], full[v, :, source], preferred_element_type=jnp.float32
+                left_factor[...], full[:, source], preferred_element_type=jnp.float32
             ).astype(stage.dtype)
 
-        write(slot, v, who).start()
-
-    pl.loop(0, nvars)(lambda v: fetch(v).start())
-
-    @pl.loop(0, nvars)
-    def _(v):
-        fetch(v).wait()
-        pl.when(has_left)(lambda: to_left(v, me).start())
-        pl.when(has_right)(lambda: to_right(v, me).start())
-
-    pl.loop(0, nvars)(lambda v: rebuild(2, v, me, v == 0))
-    write(2, 0, me).wait()
-
-    for hop in range(1, n):
+        write(slot, who).start()
+
+    pl.loop(0, chunks)(lambda c: fetch(c).start())
+
+    @pl.loop(0, chunks)
+    def _(c):
+        fetch(c).wait()
+        pl.when(has_left)(lambda: to_left(c, me).start())
+        pl.when(has_right)(lambda: to_right(c, me).start())
+
+    rebuild(0, me)
+    write(0, me).wait()
+
+    @pl.loop(1, n)
+    def _(hop):
         from_left, from_right = me - hop, me + hop
         left_ok, right_ok = from_left >= 0, from_right < n
 
-        @pl.loop(0, nvars)
-        def _(v):
+        @pl.loop(0, chunks)
+        def _(c):
             @pl.when(left_ok)
             def _():
-                to_right(v, from_left).wait_recv()
-                pl.when(has_right)(lambda: to_right(v, from_left).start())
+                to_right(c, from_left).wait_recv()
+                pl.when(has_right)(lambda: to_right(c, from_left).start())
 
             @pl.when(right_ok)
             def _():
-                to_left(v, from_right).wait_recv()
-                pl.when(has_left)(lambda: to_left(v, from_right).start())
-
-            pl.when(left_ok)(lambda: rebuild(0, v, from_left, v == 0))
-            pl.when(right_ok)(lambda: rebuild(1, v, from_right, v == 0))
-
-        pl.when(left_ok)(lambda: write(0, 0, from_left).wait())
-        pl.when(right_ok)(lambda: write(1, 0, from_right).wait())
-
-    for hop in range(n):
+                to_left(c, from_right).wait_recv()
+                pl.when(has_left)(lambda: to_left(c, from_right).start())
+
+        pl.when(left_ok)(lambda: rebuild(0, from_left))
+        pl.when(right_ok)(lambda: rebuild(1, from_right))
+        pl.when(left_ok)(lambda: write(0, from_left).wait())
+        pl.when(right_ok)(lambda: write(1, from_right).wait())
+
+    @pl.loop(0, n)
+    def _(hop):
         from_left, from_right = me - hop, me + hop
 
-        @pl.loop(0, nvars)
-        def _(v):
-            pl.when((from_left >= 0) & has_right)(lambda: to_right(v, from_left).wait_send())
-            pl.when((from_right < n) & has_left)(lambda: to_left(v, from_right).wait_send())
-
-
-def rebuild_all(core, left_factor, n):
-    nvars, depth, share = core.shape
-    rows = left_factor.shape[1]
+        @pl.loop(0, chunks)
+        def _(c):
+            pl.when((from_left >= 0) & has_right)(lambda: to_right(c, from_left).wait_send())
+            pl.when((from_right < n) & has_left)(lambda: to_left(c, from_right).wait_send())
+
+
+def rebuild_all(core, left_factor, n, number):
+    packed, share = core.shape
+    rows = left_factor.shape[0]
+    chunks = packed // CHUNK
     return pl.pallas_call(
         functools.partial(rebuild_kernel, n),
-        out_shape=jax.ShapeDtypeStruct((nvars, rows, share * n), core.dtype),
+        out_shape=jax.ShapeDtypeStruct((rows, share * n), core.dtype),
         in_specs=[ANY, VMEM],
         out_specs=ANY,
         scratch_shapes=[
-            pltpu.VMEM((nvars, depth, share * n), core.dtype),
-            pltpu.VMEM((3, rows, share), core.dtype),
-            pltpu.SemaphoreType.DMA((2, nvars, n)),
-            pltpu.SemaphoreType.DMA((nvars, n)),
-            pltpu.SemaphoreType.DMA((nvars,)),
-            pltpu.SemaphoreType.DMA((3,)),
+            pltpu.VMEM((packed, share * n), core.dtype),
+            pltpu.VMEM((2, rows, share), core.dtype),
+            pltpu.SemaphoreType.DMA((2, chunks, n)),
+            pltpu.SemaphoreType.DMA((chunks, n)),
+            pltpu.SemaphoreType.DMA((chunks,)),
+            pltpu.SemaphoreType.DMA((2,)),
         ],
         compiler_params=pltpu.CompilerParams(
-            collective_id=2, has_side_effects=True, vmem_limit_bytes=48 * 2**20
+            collective_id=2 + number, has_side_effects=True, vmem_limit_bytes=48 * 2**20
         ),
-        name="rebuild_all",
+        name=f"rebuild_all_{packed}",
     )(core, left_factor)
+
+
+def project(number, packed, n, dims, basis, rank, fibres):
+    nvars, rows, depth, width = dims
+    end = jnp.cumsum(rank)
+    begin = end - rank
+    place = jnp.arange(packed, dtype=jnp.int32)
+    owned = (place[None, :] >= begin[:, None]) & (place[None, :] < end[:, None])
+    column = jnp.sum(jnp.where(owned, place[None, :] - begin[:, None], 0), axis=0)
+    pick = (jnp.arange(basis.shape[1], dtype=jnp.int32)[:, None] == column[None, :]) & jnp.any(
+        owned, axis=0
+    )[None, :]
+    chosen = jnp.dot(
+        basis.astype(jnp.bfloat16), pick.astype(jnp.bfloat16), preferred_element_type=jnp.float32
+    ).astype(jnp.bfloat16)
+    mask = owned.astype(jnp.bfloat16)[:, None, :]
+    core = jnp.einsum(
+        "vim,vic->mc", chosen[None] * mask, fibres, preferred_element_type=jnp.float32
+    ).astype(jnp.bfloat16)
+    own = lax.dynamic_slice_in_dim(chosen, lax.axis_index("fib") * rows, rows, 0)
+    left_factor = (own[None] * mask).reshape(nvars * rows, packed)
+    return rebuild_all(core, left_factor, n, number).reshape(dims)
 
 
 def highest(a, b, dims):
@@ -380,7 +412,7 @@
 
 
 def iterate_kernel(gram, start, basis):
-    basis[...] = orthonormal(start[...])
+    basis[...] = start[...]
 
     @pl.loop(0, ITERS)
     def _(step):
@@ -401,19 +433,19 @@
 def on_device(sizes, field, rank, start_basis):
     nvars, rows, depth, width = field.shape
     n = sizes["fib"]
+    needed = lax.pmax(jnp.sum(rank), tuple(sizes))
     flat = field.reshape(nvars, rows, depth * width)
-    fibres, partial_gram = exchange(flat, n)
+    fibres, partial_gram, basis = exchange(flat, start_basis, n)
     gram = reduce_all(partial_gram, tuple((axis, sizes[axis]) for axis in ("var", "slab", "fib")))
-    basis = iterate(gram, start_basis)
-    columns = jnp.arange(basis.shape[1], dtype=jnp.int32)
-    keep = (columns[None, :] < rank[:, None]).astype(basis.dtype)
-    basis_bf = (basis[None, :, :] * keep[:, None, :]).astype(jnp.bfloat16)
-    core = jnp.einsum("vir,vic->vrc", basis_bf, fibres, preferred_element_type=jnp.float32).astype(
-        jnp.bfloat16
-    )
-    own_rows = lax.dynamic_slice_in_dim(basis_bf, lax.axis_index("fib") * rows, rows, 1)
-    result = rebuild_all(core, own_rows, n)
-    return result.reshape(nvars, rows, depth, width)
+    basis = iterate(gram, basis)
+    most = nvars * basis.shape[1]
+    widths = sorted({max(CHUNK, most * part // 16 // CHUNK * CHUNK) for part in PARTS})
+    branches = [
+        functools.partial(project, number, packed, n, field.shape)
+        for number, packed in enumerate(widths)
+    ]
+    choice = sum((needed > packed).astype(jnp.int32) for packed in widths[:-1])
+    return lax.switch(choice, branches, basis, rank, fibres)
 
 
 def solution(mesh):

time: 826 us -> 827 us (level)
  Pallas kernels: 764 us -> 684 us
  blocking collectives: 0 us -> 42.2 us
  loops' own time: 0 us -> 19.5 us
    pallas_call x1, Pallas kernels: 277 us -> 215 us  [rebuild_all(): pl.pallas_call(functools.partial(rebuild_kernel, n), out_shape=jax.ShapeD...]
    pmax x0 -> x1, blocking collectives: none -> 42.2 us  [on_device(): needed = lax.pmax(jnp.sum(rank), tuple(sizes))]
    another operation x0 -> x1, loops' own time: none -> 19.5 us  [on_device(): return lax.switch(choice, branches, basis, rank, fibres)]
    pallas_call x1, Pallas kernels: 87.9 us -> 71.6 us  [iterate(): pl.pallas_call(iterate_kernel, out_shape=jax.ShapeDtypeStruct(start.shape...]
    unnamed x9 -> x8, local copies, waits for them, and re-layouts: 24 us -> 11.9 us
    cond x0 -> x1, local copies, waits for them, and re-layouts: none -> 10.3 us
    dot_general x1 -> x2, matrix products: 10.2 us -> 17.3 us  [the longest x1 16.9 us: project(): jnp.einsum('vim,vic->mc', chosen[None] * mask, fibres, preferred_element_...]
where the time goes in v3:
time: 827 us; the launch traced here: 818 us
  Pallas kernels  684 us (83%)
  local copies, waits for them, and re-layouts  48 us (6%)
  blocking collectives  42.2 us (5%)
  loops' own time  19.5 us (2%)
  matrix products  17.3 us (2%)
    pallas_call x1, Pallas kernels, exchange(): pl.pallas_call(functools.partial(exchange_kernel, n), out_shape=(jax.Shap...  357 us
    pallas_call x1, Pallas kernels, rebuild_all(): pl.pallas_call(functools.partial(rebuild_kernel, n), out_shape=jax.ShapeD...  215 us
    pallas_call x1, Pallas kernels, iterate(): pl.pallas_call(iterate_kernel, out_shape=jax.ShapeDtypeStruct(start.shape...  71.6 us
    pmax x1, blocking collectives, on_device(): needed = lax.pmax(jnp.sum(rank), tuple(sizes))  42.2 us
    pallas_call x1, Pallas kernels, reduce_all(): pl.pallas_call(functools.partial(reduce_kernel, axes), out_shape=jax.Shap...  40.7 us
    reshape x1, local copies, waits for them, and re-layouts, on_device(): flat = field.reshape(nvars, rows, depth * width)  25.6 us
    another operation x1, loops' own time, on_device(): return lax.switch(choice, branches, basis, rank, fibres)  19.5 us
    dot_general x1, matrix products, project(): jnp.einsum('vim,vic->mc', chosen[None] * mask, fibres, preferred_element_...  16.9 us

profile of v3, /device:TPU:0, one launch (start us, length us, event | category | flops | bytes accessed | tf_op | source)
XLA Modules:
  0.0 818.2 jit_solution(5674223931170466073)
XLA Ops:
  0.0 1.3 reduce_sum.90
  1.3 42.2 %pmax.7 = s32[]{:T(128)} all-reduce(s32[]{:T(128)} %reduce_sum.90), channel_id=1, replica_groups=mesh['grp'=2,'fib'=4,'slab'=2,'var'=2] {'grp','fib','slab','var'}, use_global_device_ids=true, to_apply=%region_1.0 | all-reduce | flops 1 | bytes 8 | tf_op jit(solution)/shard_map/pmax | solution.py:436
  48.7 0.0 copy-start.2
  48.7 25.6 %reshape.624.flat = bf16[8,128,8192]{2,1,0:T(8,128)(2,1)} reshape(bf16[8,128,32,256]{3,2,1,0:T(8,128)(2,1)} %param.12) | data formatting | bytes 33554432 | tf_op jit(solution)/shard_map/reshape | solution.py:437
  74.3 0.0 copy-done.2
  74.3 0.0 copy-start
  74.3 5.8 copy-done
  80.1 0.0 copy-start.4
  80.1 356.7 %exchange.1 = (bf16[8,512,2048]{2,1,0:T(8,128)(2,1)}, f32[512,512]{1,0:T(8,128)S(1)}, f32[512,128]{1,0:T(8,128)S(1)}) custom-call(bf16[8,128,8192]{2,1,0:T(8,128)(2,1)S(1)} %copy-done, f32[512,128]{1,0:T(8,128)S(1)} %copy-done.2), custom_call_target="tpu_custom_call" | custom-call | tf_op jit(solution)/shard_map/exchange/pallas_call | solution.py:100
  436.8 40.7 %reduce_all.1.gram = f32[512,512]{1,0:T(8,128)S(1)} custom-call(f32[512,512]{1,0:T(8,128)S(1)} %get-tuple-element.99.part), custom_call_target="tpu_custom_call" | custom-call | tf_op jit(solution)/shard_map/reduce_all/pallas_call | solution.py:209
  477.5 71.6 %iterate.1 = f32[512,128]{1,0:T(8,128)S(1)} custom-call(f32[512,512]{1,0:T(8,128)S(1)} %reduce_all.1.gram, f32[512,128]{1,0:T(8,128)S(1)} %get-tuple-element.100.start), custom_call_target="tpu_custom_call" | custom-call | tf_op jit(solution)/shard_map/iterate/pallas_call | solution.py:423
  549.2 0.0 copy-done.4
  549.2 262.6 %conditional.1 = (bf16[8,128,32,256]{3,2,1,0:T(8,128)(2,1)S(1)}) conditional(s32[]{:T(128)} %clamp.3, (s32[8]{0:T(128)S(1)}, f32[512,128]{1,0:T(8,128)S(1)}, bf16[8,512,2048]{2,1,0:T(8,128)(2,1)}) %tuple.61, (s32[8]{0:T(128)S(1)}, f32[512,128]{1,0:T(8,128)S(1)}, bf16[8,512,2048]{2,1,0:T(8,128)(2,1)}) %tuple.62, ...), branch_computations={%region_2.6_spmd, %region_6.10_spmd, %region_10.14_spmd, %region_1... | conditional | flops 17322498048 | bytes 73813144 | solution.py:448
  561.1 0.2 reduce-window.68
  561.3 0.1 select_reduce_fusion.5
  561.3 0.1 fusion.89
  561.4 0.4 convolution_convert_fusion.5
  561.8 16.9 %bitcast_convert_fusion.5.core = bf16[768,2048]{1,0:T(8,128)(2,1)S(1)} fusion(bf16[8,512,2048]{2,1,0:T(8,128)(2,1)} %get-tuple-element.86, bf16[8,768]{1,0:T(8,128)(2,1)S(1)} %get-tuple-element.114, bf16[512,768]{0,1:T(8,128)(2,1)S(1)} %bitcast.149), kind=kOutput, calls=%fused_computation.105 | convolution fusion | flops 12889620480 | bytes 20721664 | tf_op jit(solution)/shard_map/cond/branch_5_fun/vim,vic->mc/dot_general | solution.py:364
  578.8 0.1 copy.18
  579.0 0.1 broadcast_multiply_fusion.5
  579.1 214.8 %rebuild_all_768.1 = bf16[1024,8192]{1,0:T(8,128)(2,1)} custom-call(bf16[768,2048]{1,0:T(8,128)(2,1)S(1)} %bitcast_convert_fusion.5.core, bf16[1024,768]{1,0:T(8,128)(2,1)S(1)} %bitcast.123), custom_call_target="tpu_custom_call" | custom-call | tf_op jit(solution)/shard_map/cond/branch_5_fun/rebuild_all_768/pallas_call | solution.py:330
  793.9 10.3 %copy.27 = bf16[128,8,32,256]{3,2,1,0:T(8,128)(2,1)S(1)} copy(bf16[128,8,32,256]{3,1,2,0:T(8,128)(2,1)} %bitcast.133) | data formatting | bytes 33554432 | tf_op jit(solution)/shard_map/cond
  811.8 0.0 copy-start.3
  811.8 6.2 copy-done.3
  (2 shorter events, 0.0 us)
Async XLA Ops:
  48.7 25.6 %copy-start.2 = (f32[512,128]{1,0:T(8,128)S(1)}, f32[512,128]{1,0:T(8,128)}, u32[]{:S(2)}) copy-start(f32[512,128]{1,0:T(8,128)} %start_basis.1) | copy-start | bytes 786436
  74.3 5.8 copy-start
  80.1 469.1 %copy-start.4 = (s32[8]{0:T(128)S(1)}, s32[8]{0:T(128)}, u32[]{:S(2)}) copy-start(s32[8]{0:T(128)} %param.13) | copy-start | bytes 100
  811.8 6.2 copy-start.3

commit v4 on v2

--- a/solution.py
+++ b/solution.py
@@ -21,7 +21,7 @@
     pl.semaphore_wait(barrier, len(peers))
 
 
-def exchange_kernel(n, flat, fibres, gram, held, send_sem, recv_sem, own_sem, load_sem):
+def exchange_kernel(n, flat, start_basis, fibres, gram, basis, held, send_sem, recv_sem, own_sem, load_sem):
     nvars, rows, _ = flat.shape
     share = fibres.shape[2]
     tile = min(share, 512)
@@ -82,13 +82,17 @@
                 block, block, (((1,), (1,)), ((), ())), preferred_element_type=jnp.float32
             )
 
-    @pl.loop(0, nvars + WINDOW)
+    first = min(WINDOW, nvars)
+    pl.loop(0, first)(start)
+    basis[...] = orthonormal(start_basis[...])
+
+    @pl.loop(first, nvars + WINDOW)
     def _(step):
         pl.when(step < nvars)(lambda: start(step))
         pl.when(step >= WINDOW)(lambda: finish(step - WINDOW))
 
 
-def exchange(flat, n):
+def exchange(flat, start_basis, n):
     nvars, rows, columns = flat.shape
     whole, share = rows * n, columns // n
     return pl.pallas_call(
@@ -96,9 +100,10 @@
         out_shape=(
             jax.ShapeDtypeStruct((nvars, whole, share), flat.dtype),
             jax.ShapeDtypeStruct((whole, whole), jnp.float32),
+            jax.ShapeDtypeStruct(start_basis.shape, jnp.float32),
         ),
-        in_specs=[ANY],
-        out_specs=(ANY, VMEM),
+        in_specs=[ANY, VMEM],
+        out_specs=(ANY, VMEM, VMEM),
         scratch_shapes=[
             pltpu.VMEM((whole, share), flat.dtype),
             pltpu.SemaphoreType.DMA((nvars, n)),
@@ -110,7 +115,7 @@
             collective_id=0, has_side_effects=True, vmem_limit_bytes=32 * 2**20
         ),
         name="exchange",
-    )(flat)
+    )(flat, start_basis)
 
 
 def reduce_kernel(axes, part, total, held, *scratch):
@@ -380,7 +385,7 @@
 
 
 def iterate_kernel(gram, start, basis):
-    basis[...] = orthonormal(start[...])
+    basis[...] = start[...]
 
     @pl.loop(0, ITERS)
     def _(step):
@@ -402,9 +407,9 @@
     nvars, rows, depth, width = field.shape
     n = sizes["fib"]
     flat = field.reshape(nvars, rows, depth * width)
-    fibres, partial_gram = exchange(flat, n)
+    fibres, partial_gram, basis = exchange(flat, start_basis, n)
     gram = reduce_all(partial_gram, tuple((axis, sizes[axis]) for axis in ("var", "slab", "fib")))
-    basis = iterate(gram, start_basis)
+    basis = iterate(gram, basis)
     columns = jnp.arange(basis.shape[1], dtype=jnp.int32)
     keep = (columns[None, :] < rank[:, None]).astype(basis.dtype)
     basis_bf = (basis[None, :, :] * keep[:, None, :]).astype(jnp.bfloat16)

time: 826 us -> 805 us (0.975)
  Pallas kernels: 764 us -> 748 us
    pallas_call x1, Pallas kernels: 87.9 us -> 71.8 us  [iterate(): pl.pallas_call(iterate_kernel, out_shape=jax.ShapeDtypeStruct(start.shape...]
    unnamed x9 -> x7, local copies, waits for them, and re-layouts: 24 us -> 21.8 us
where the time goes in v4:
time: 805 us; the launch traced here: 804 us
  Pallas kernels  748 us (93%)
  local copies, waits for them, and re-layouts  47.4 us (6%)
  matrix products  8.21 us (1%)
    pallas_call x1, Pallas kernels, exchange(): pl.pallas_call(functools.partial(exchange_kernel, n), out_shape=(jax.Shap...  358 us
    pallas_call x1, Pallas kernels, rebuild_all(): pl.pallas_call(functools.partial(rebuild_kernel, n), out_shape=jax.ShapeD...  277 us
    pallas_call x1, Pallas kernels, iterate(): pl.pallas_call(iterate_kernel, out_shape=jax.ShapeDtypeStruct(start.shape...  71.8 us
    pallas_call x1, Pallas kernels, reduce_all(): pl.pallas_call(functools.partial(reduce_kernel, axes), out_shape=jax.Shap...  41.8 us
    reshape x1, local copies, waits for them, and re-layouts, on_device(): flat = field.reshape(nvars, rows, depth * width)  25.6 us
    unnamed x7, local copies, waits for them, and re-layouts  21.8 us

profile of v4, /device:TPU:0, one launch (start us, length us, event | category | flops | bytes accessed | tf_op | source)
XLA Modules:
  0.0 804.3 jit_solution(12832434506986539456)
XLA Ops:
  0.0 0.0 copy-start.1
  0.0 25.6 %reshape.25.flat = bf16[8,128,8192]{2,1,0:T(8,128)(2,1)} reshape(bf16[8,128,32,256]{3,2,1,0:T(8,128)(2,1)} %param.3) | data formatting | bytes 33554432 | tf_op jit(solution)/shard_map/reshape | solution.py:409
  25.6 0.0 copy-done.1
  25.6 0.0 copy-start.2
  25.6 357.5 %exchange.1 = (bf16[8,512,2048]{2,1,0:T(8,128)(2,1)S(1)}, f32[512,512]{1,0:T(8,128)S(1)}, f32[512,128]{1,0:T(8,128)S(1)}) custom-call(bf16[8,128,8192]{2,1,0:T(8,128)(2,1)} %reshape.25.flat, f32[512,128]{1,0:T(8,128)S(1)} %copy-done.1), custom_call_target="tpu_custom_call" | custom-call | tf_op jit(solution)/shard_map/exchange/pallas_call | solution.py:98
  383.1 0.0 copy-start
  383.1 6.2 copy-done
  389.3 41.8 %reduce_all.1.gram = f32[512,512]{1,0:T(8,128)S(1)} custom-call(f32[512,512]{1,0:T(8,128)S(1)} %get-tuple-element.8.part), custom_call_target="tpu_custom_call" | custom-call | tf_op jit(solution)/shard_map/reduce_all/pallas_call | solution.py:207
  431.1 71.8 %iterate.1 = f32[512,128]{1,0:T(8,128)S(1)} custom-call(f32[512,512]{1,0:T(8,128)S(1)} %reduce_all.1.gram, f32[512,128]{1,0:T(8,128)S(1)} %get-tuple-element.9.start), custom_call_target="tpu_custom_call" | custom-call | tf_op jit(solution)/shard_map/iterate/pallas_call | solution.py:396
  502.9 0.0 copy-done.2
  503.0 0.1 fusion
  503.0 0.2 multiply_convert_fusion
  503.3 8.2 %convolution_convert_fusion.core = bf16[8,128,2048]{2,1,0:T(8,128)(2,1)S(1)} fusion(bf16[8,512,2048]{2,1,0:T(8,128)(2,1)} %copy-done, f32[8,128]{1,0:T(8,128)S(1)} %fusion, f32[512,128]{1,0:T(8,128)S(1)} %iterate.1), kind=kOutput, calls=%fused_computation | convolution fusion | flops 2150629376 | bytes 21237760 | tf_op jit(solution)/shard_map/vir,vic->vrc/dot_general | solution.py:416
  511.5 277.2 %rebuild_all.1 = bf16[8,128,8192]{2,1,0:T(8,128)(2,1)} custom-call(bf16[8,128,2048]{2,1,0:T(8,128)(2,1)S(1)} %convolution_convert_fusion.core, bf16[8,128,128]{2,1,0:T(8,128)(2,1)S(1)} %constant_dynamic-slice_fusion.left_factor), custom_call_target="tpu_custom_call" | custom-call | tf_op jit(solution)/shard_map/rebuild_all/pallas_call | solution.py:325
  788.7 15.6 %copy.6 = bf16[128,8,32,256]{3,2,1,0:T(8,128)(2,1)} copy(bf16[128,8,32,256]{3,1,2,0:T(8,128)(2,1)} %bitcast.7) | data formatting | bytes 33554432
  (1 shorter events, 0.0 us)
Async XLA Ops:
  0.0 25.6 %copy-start.1 = (f32[512,128]{1,0:T(8,128)S(1)}, f32[512,128]{1,0:T(8,128)}, u32[]{:S(2)}) copy-start(f32[512,128]{1,0:T(8,128)} %start_basis.1) | copy-start | bytes 786436
  25.6 477.4 %copy-start.2 = (s32[8]{0:T(128)S(1)}, s32[8]{0:T(128)}, u32[]{:S(2)}) copy-start(s32[8]{0:T(128)} %param.4) | copy-start | bytes 100
  383.1 6.2 copy-start
